TPU v7x, 256 devices: a whole 4x4x8 slice. The times are simulated.
256 devices in a mesh: depth: 4 (over x), gx: 16 (over z, core), gy: 4 (over y).
Axes of the slice: x: 4, y: 4, z: 8, core: 2. Of those that a mesh axis runs over, the one named last changes fastest.
Arguments:
- density: float32 [16, 512, 1024], P('depth', 'gx', 'gy'), may hold values from 0.1 to 1
- table_index: int32 [16, 512, 1024], P('depth', 'gx', 'gy'), may hold values from 0 to 255
- opacity_table: float32 [256], replicated, may hold values from 0.02 to 0.3
- color_table: float32 [3, 256], replicated, may hold values from 0.5 to 3
- light_direction: float32 [4, 3], replicated, may hold values from -4 to 4
- shear_offsets: int32 [4, 16, 2], replicated, may hold values from -16 to 16, as said below
Outputs:
- image: float32 [4, 4, 512, 1024], P('depth', None, 'gx', 'gy')
Inputs may be any that keep to these rules, and one draw needn't show every extreme that they name: `shear_offsets`: every offset lies within -16 to 16; both ends occur in every draw.
All inputs are finite; a program needn't handle non-finite values.
Results may differ from a plain program's by a relative error of at most 0.000051.
Values sent between devices are 32-bit elements; how exact they have to be, the bound alone decides.
No kernel may reach another device: no remote copies, remote signals or barrier semaphores. Data moves between devices by JAX's collectives and lax.ppermute only.
A program may use at most 64 MiB of HBM per device.

v0:
```python
import jax
import jax.numpy as jnp
from jax import lax
from jax.sharding import PartitionSpec as P

VIEWS = 4
MAXS = 16


ambient = 0.3
diffuse = 0.7


def with_halo(block, sides, width):
    for axis, dim in sides:
        count = lax.axis_size(axis)
        forward = [(i, i + 1) for i in range(count - 1)]
        backward = [(target, source) for source, target in forward]
        low = lax.ppermute(
            lax.slice_in_dim(block, block.shape[dim] - width, None, axis=dim), axis, forward
        )
        high = lax.ppermute(lax.slice_in_dim(block, 0, width, axis=dim), axis, backward)
        block = jnp.concatenate([low, block, high], axis=dim)
    return block


def swapped(value, axis, stride):
    mask = 2**stride
    pairs = [(source, source ^ mask) for source in range(lax.axis_size(axis))]
    return lax.ppermute(value, axis, pairs)


def table_lookup(index_block, opacity_table, color_table):
    tables = jnp.concatenate([opacity_table[None], color_table], axis=0)
    entries = tables.shape[1]
    slices, rows, cols = index_block.shape
    codes = lax.broadcasted_iota(jnp.int32, (entries, 1), 0)
    looked = []
    for slice_pos in range(slices):
        flat_index = index_block[slice_pos].reshape(1, rows * cols)
        onehot = (codes == flat_index).astype(jnp.float32)
        values = jnp.dot(
            tables, onehot, precision=lax.Precision.HIGHEST, preferred_element_type=jnp.float32
        )
        looked.append(values.reshape(4, rows, cols))
    stacked = jnp.stack(looked, axis=1)
    return (stacked[0], stacked[1:])


def shade_block(padded, index_block, opacity_table, color_table):
    slope_depth = 0.5 * (padded[2:, 1:-1, 1:-1] - padded[:-2, 1:-1, 1:-1])
    slope_row = 0.5 * (padded[1:-1, 2:, 1:-1] - padded[1:-1, :-2, 1:-1])
    slope_col = 0.5 * (padded[1:-1, 1:-1, 2:] - padded[1:-1, 1:-1, :-2])
    inner = padded[1:-1, 1:-1, 1:-1]
    kappa, colors = table_lookup(index_block, opacity_table, color_table)
    alpha = 1.0 - jnp.exp(-kappa * inner)
    base = alpha[None] * colors
    lengths = jnp.sqrt(
        slope_depth * slope_depth + slope_row * slope_row + slope_col * slope_col + 1.0
    )
    return (slope_depth, slope_row, slope_col, lengths, alpha, base)


def fragment_of(shaded, light):
    slope_depth, slope_row, slope_col, lengths, alpha, base = shaded
    lambert = (
        jnp.abs(light[0] * slope_depth + light[1] * slope_row + light[2] * slope_col) / lengths
    )
    return jnp.concatenate([alpha[None], base * (ambient + diffuse * lambert)[None]], axis=0)


def composite_view(framed, shear_row, first_slice, rows, cols):
    accum = jnp.zeros((4, rows, cols), jnp.float32)
    for slice_pos in range(framed.shape[1]):
        offset_pair = lax.dynamic_index_in_dim(
            shear_row, first_slice + slice_pos, 0, keepdims=False
        )
        starts = (jnp.int32(0), MAXS - offset_pair[0], MAXS - offset_pair[1])
        shifted = lax.dynamic_slice(framed[:, slice_pos], starts, (4, rows, cols))
        accum = accum + (1.0 - accum[0:1]) * shifted
    return accum


def over(front, back):
    return front + (1.0 - front[:, 0:1]) * back


def local(density, table_index, opacity_table, color_table, light_direction, shear_offsets):
    slices, rows, cols = density.shape
    depth_pos = lax.axis_index("depth")
    first_slice = depth_pos * slices
    views_done = []
    padded = with_halo(density, (("depth", 0), ("gx", 1), ("gy", 2)), 1)
    shaded = shade_block(padded, table_index, opacity_table, color_table)
    for view_number in range(VIEWS):
        fragment = fragment_of(shaded, light_direction[view_number])
        framed = with_halo(fragment, (("gx", 2), ("gy", 3)), MAXS)
        views_done.append(
            composite_view(framed, shear_offsets[view_number], first_slice, rows, cols)
        )
    partial_value = jnp.stack(views_done)
    current = partial_value
    bit_count = lax.axis_size("depth").bit_length() - 1
    for bit in range(bit_count):
        remaining = current.shape[0]
        paired = current.reshape(remaining // 2, 2, 4, rows, cols)
        upper_half = depth_pos // 2**bit % 2 == 1
        kept = jnp.where(upper_half, paired[:, 1], paired[:, 0])
        given = jnp.where(upper_half, paired[:, 0], paired[:, 1])
        received = swapped(given, "depth", bit)
        current = jnp.where(upper_half, over(received, kept), over(kept, received))
    return current


def solution(mesh):
    return jax.shard_map(
        local,
        mesh=mesh,
        in_specs=(P("depth", "gx", "gy"), P("depth", "gx", "gy"), P(), P(), P(), P()),
        out_specs=P("depth", None, "gx", "gy"),
        check_vma=False,
    )
```

profile of v0, /device:TPU:124, one launch (start us, length us, event | category | flops | bytes accessed | tf_op | source)
XLA Modules:
  0.0 194.3 jit_solution(9722172530349932680)
XLA Ops:
  0.8 3.1 %collective-permute-start.1 = (f32[1,32,256]{2,1,0:T(8,128)S(1)}, f32[1,32,256]{2,1,0:T(8,128)S(1)}, u32[]{:S(2)}, u32[]{:S(2)}) collective-permute-start(f32[1,32,256]{2,1,0:T(8,128)S(1)} %get-tuple-element.64), channel_id=1, source_target_pairs={{0,64},{64,128},{128,192},{1,65},{65,129},{129,193},{2,66},{66,130... | collective-permute-start | bytes 98312 | tf_op jit(solution)/shard_map/ppermute | solution.py:19
  3.9 2.7 %collective-permute-start = (f32[1,32,256]{2,1,0:T(8,128)S(1)}, f32[1,32,256]{2,1,0:T(8,128)S(1)}, u32[]{:S(2)}, u32[]{:S(2)}) collective-permute-start(f32[1,32,256]{2,1,0:T(8,128)S(1)} %get-tuple-element.63), channel_id=1, source_target_pairs={{64,0},{128,64},{192,128},{65,1},{129,65},{193,129},{66,2},{130,66... | collective-permute-start | bytes 98312 | tf_op jit(solution)/shard_map/ppermute | solution.py:22
  9.4 3.4 %fusion.3 = f32[4,8192]{1,0:T(4,128)S(1)} fusion(s32[8192]{0:T(1024)S(1)} %bitcast.298, f32[3,256]{1,0:T(4,128)} %param.9, f32[1,256]{1,0:T(1,128)} %bitcast.302), kind=kOutput, calls=%fused_computation.7 | convolution fusion | flops 102761472 | bytes 167936 | tf_op jit(solution)/shard_map/dot_general | solution.py:42
  12.7 2.7 %fusion.2 = f32[4,8192]{1,0:T(4,128)S(1)} fusion(s32[8192]{0:T(1024)S(1)} %bitcast.299, f32[3,256]{1,0:T(4,128)S(1)} %copy-done.2, f32[1,256]{1,0:T(1,128)S(1)} %bitcast.303), kind=kOutput, calls=%fused_computation.6 | convolution fusion | flops 102761472 | bytes 167936 | tf_op jit(solution)/shard_map/dot_general | solution.py:42
  15.4 2.7 %fusion.1 = f32[4,8192]{1,0:T(4,128)S(1)} fusion(s32[8192]{0:T(1024)S(1)} %bitcast.300, f32[3,256]{1,0:T(4,128)S(1)} %copy-done.2, f32[1,256]{1,0:T(1,128)S(1)} %bitcast.304), kind=kOutput, calls=%fused_computation.5 | convolution fusion | flops 102761472 | bytes 167936 | tf_op jit(solution)/shard_map/dot_general | solution.py:42
  18.1 2.7 %fusion = f32[4,8192]{1,0:T(4,128)S(1)} fusion(s32[8192]{0:T(1024)S(1)} %bitcast.301, f32[3,256]{1,0:T(4,128)S(1)} %copy-done.2, f32[1,256]{1,0:T(1,128)S(1)} %bitcast.305), kind=kOutput, calls=%fused_computation.4 | convolution fusion | flops 102761472 | bytes 167936 | tf_op jit(solution)/shard_map/dot_general | solution.py:42
  28.1 3.6 %collective-permute-start.2 = (f32[6,1,256]{2,1,0:T(1,128)S(1)}, f32[6,1,256]{2,1,0:T(1,128)S(1)}, u32[]{:S(2)}, u32[]{:S(2)}) collective-permute-start(f32[6,1,256]{2,1,0:T(1,128)S(1)} %get-tuple-element.46), channel_id=1, source_target_pairs={{4,0},{8,4},{12,8},{16,12},{20,16},{24,20},{28,24},{32,28},{36,32}... | collective-permute-start | bytes 18440 | tf_op jit(solution)/shard_map/ppermute | solution.py:22
  36.4 4.6 %collective-permute-start.4 = (f32[6,34,1]{2,1,0:T(8,128)S(1)}, f32[6,34,1]{2,1,0:T(8,128)S(1)}, u32[]{:S(2)}, u32[]{:S(2)}) collective-permute-start(f32[6,34,1]{2,1,0:T(8,128)S(1)} %get-tuple-element.44), channel_id=1, source_target_pairs={{1,0},{2,1},{3,2},{5,4},{6,5},{7,6},{9,8},{10,9},{11,10},{13,12},{... | collective-permute-start | bytes 2456 | tf_op jit(solution)/shard_map/ppermute | solution.py:22
  50.2 4.1 %collective-permute-start.6 = (f32[4,4,16,256]{3,2,1,0:T(8,128)S(1)}, f32[4,4,16,256]{3,2,1,0:T(8,128)S(1)}, u32[]{:S(2)}, u32[]{:S(2)}) collective-permute-start(f32[4,4,16,256]{3,2,1,0:T(8,128)S(1)} %get-tuple-element.34), channel_id=1, source_target_pairs={{0,4},{4,8},{8,12},{12,16},{16,20},{20,24},{24,28},{28,32},{32,36}... | collective-permute-start | bytes 786440 | tf_op jit(solution)/shard_map/ppermute | solution.py:19
  58.0 4.8 %collective-permute-start.10 = (f32[4,4,16,256]{3,2,1,0:T(8,128)}, f32[4,4,16,256]{3,2,1,0:T(8,128)S(1)}, u32[]{:S(2)}, u32[]{:S(2)}) collective-permute-start(f32[4,4,16,256]{3,2,1,0:T(8,128)} %get-tuple-element.56), channel_id=1, source_target_pairs={{0,4},{4,8},{8,12},{12,16},{16,20},{20,24},{24,28},{28,32},{32,36}... | collective-permute-start | bytes 786440 | tf_op jit(solution)/shard_map/ppermute | solution.py:19
  64.8 4.9 %collective-permute-start.14 = (f32[4,4,16,256]{3,2,1,0:T(8,128)}, f32[4,4,16,256]{3,2,1,0:T(8,128)}, u32[]{:S(2)}, u32[]{:S(2)}) collective-permute-start(f32[4,4,16,256]{3,2,1,0:T(8,128)} %get-tuple-element.58), channel_id=1, source_target_pairs={{0,4},{4,8},{8,12},{12,16},{16,20},{20,24},{24,28},{28,32},{32,36}... | collective-permute-start | bytes 786440 | tf_op jit(solution)/shard_map/ppermute | solution.py:19
  71.6 4.9 %collective-permute-start.18 = (f32[4,4,16,256]{3,2,1,0:T(8,128)}, f32[4,4,16,256]{3,2,1,0:T(8,128)S(1)}, u32[]{:S(2)}, u32[]{:S(2)}) collective-permute-start(f32[4,4,16,256]{3,2,1,0:T(8,128)} %get-tuple-element.60), channel_id=1, source_target_pairs={{0,4},{4,8},{8,12},{12,16},{16,20},{20,24},{24,28},{28,32},{32,36}... | collective-permute-start | bytes 786440 | tf_op jit(solution)/shard_map/ppermute | solution.py:19
  119.6 2.7 %collective-permute-start.21 = (f32[4,4,64,16]{3,2,1,0:T(8,128)S(1)}, f32[4,4,64,16]{3,2,1,0:T(8,128)S(1)}, u32[]{:S(2)}, u32[]{:S(2)}) collective-permute-start(f32[4,4,64,16]{3,2,1,0:T(8,128)S(1)} %get-tuple-element.30), channel_id=1, source_target_pairs={{1,0},{2,1},{3,2},{5,4},{6,5},{7,6},{9,8},{10,9},{11,10},{13,12},{... | collective-permute-start | bytes 196616 | tf_op jit(solution)/shard_map/ppermute | solution.py:22
  123.8 4.6 %collective-permute-start.9 = (f32[4,4,64,16]{3,2,1,0:T(8,128)S(1)}, f32[4,4,64,16]{3,2,1,0:T(8,128)S(1)}, u32[]{:S(2)}, u32[]{:S(2)}) collective-permute-start(f32[4,4,64,16]{3,2,1,0:T(8,128)S(1)} %get-tuple-element.24), channel_id=1, source_target_pairs={{1,0},{2,1},{3,2},{5,4},{6,5},{7,6},{9,8},{10,9},{11,10},{13,12},{... | collective-permute-start | bytes 196616 | tf_op jit(solution)/shard_map/ppermute | solution.py:22
  129.9 4.6 %collective-permute-start.13 = (f32[4,4,64,16]{3,2,1,0:T(8,128)S(1)}, f32[4,4,64,16]{3,2,1,0:T(8,128)S(1)}, u32[]{:S(2)}, u32[]{:S(2)}) collective-permute-start(f32[4,4,64,16]{3,2,1,0:T(8,128)S(1)} %get-tuple-element.26), channel_id=1, source_target_pairs={{1,0},{2,1},{3,2},{5,4},{6,5},{7,6},{9,8},{10,9},{11,10},{13,12},{... | collective-permute-start | bytes 196616 | tf_op jit(solution)/shard_map/ppermute | solution.py:22
  137.3 3.4 %collective-permute-start.17 = (f32[4,4,64,16]{3,2,1,0:T(8,128)S(1)}, f32[4,4,64,16]{3,2,1,0:T(8,128)S(1)}, u32[]{:S(2)}, u32[]{:S(2)}) collective-permute-start(f32[4,4,64,16]{3,2,1,0:T(8,128)S(1)} %get-tuple-element.28), channel_id=1, source_target_pairs={{1,0},{2,1},{3,2},{5,4},{6,5},{7,6},{9,8},{10,9},{11,10},{13,12},{... | collective-permute-start | bytes 196616 | tf_op jit(solution)/shard_map/ppermute | solution.py:22
  145.1 3.4 %collective-permute-done.8 = f32[4,4,64,16]{3,2,1,0:T(8,128)S(1)} collective-permute-done((f32[4,4,64,16]{3,2,1,0:T(8,128)S(1)}, f32[4,4,64,16]{3,2,1,0:T(8,128)S(1)}, u32[]{:S(2)}, u32[]{:S(2)}) %collective-permute-start.8) | collective-permute-done | bytes 65568 | tf_op jit(solution)/shard_map/ppermute | solution.py:19
  148.5 6.5 %collective-permute-done.13 = f32[4,4,64,16]{3,2,1,0:T(8,128)S(1)} collective-permute-done((f32[4,4,64,16]{3,2,1,0:T(8,128)S(1)}, f32[4,4,64,16]{3,2,1,0:T(8,128)S(1)}, u32[]{:S(2)}, u32[]{:S(2)}) %collective-permute-start.13) | collective-permute-done | bytes 65568 | tf_op jit(solution)/shard_map/ppermute | solution.py:22
  155.0 4.7 %collective-permute-done.12 = f32[4,4,64,16]{3,2,1,0:T(8,128)S(1)} collective-permute-done((f32[4,4,64,16]{3,2,1,0:T(8,128)S(1)}, f32[4,4,64,16]{3,2,1,0:T(8,128)S(1)}, u32[]{:S(2)}, u32[]{:S(2)}) %collective-permute-start.12) | collective-permute-done | bytes 65568 | tf_op jit(solution)/shard_map/ppermute | solution.py:19
  159.7 6.5 %collective-permute-done.17 = f32[4,4,64,16]{3,2,1,0:T(8,128)S(1)} collective-permute-done((f32[4,4,64,16]{3,2,1,0:T(8,128)S(1)}, f32[4,4,64,16]{3,2,1,0:T(8,128)S(1)}, u32[]{:S(2)}, u32[]{:S(2)}) %collective-permute-start.17) | collective-permute-done | bytes 65568 | tf_op jit(solution)/shard_map/ppermute | solution.py:22
  166.3 4.7 %collective-permute-done.16 = f32[4,4,64,16]{3,2,1,0:T(8,128)S(1)} collective-permute-done((f32[4,4,64,16]{3,2,1,0:T(8,128)S(1)}, f32[4,4,64,16]{3,2,1,0:T(8,128)S(1)}, u32[]{:S(2)}, u32[]{:S(2)}) %collective-permute-start.16) | collective-permute-done | bytes 65568 | tf_op jit(solution)/shard_map/ppermute | solution.py:19
  171.0 3.7 %fusion.11 = (f32[4,4,64,288]{3,2,1,0:T(8,128)S(1)}, f32[4,4,64,288]{3,2,1,0:T(8,128)S(1)}, f32[4,4,64,288]{3,2,1,0:T(8,128)S(1)}) fusion(f32[1,4,32,256]{3,2,1,0:T(8,128)S(1)} %bitcast.293, f32[4,4,64,16]{3,2,1,0:T(8,128)S(1)} %collective-permute-done.9, f32[4,4,16,256]{3,2,1,0:T(8,128)S(1)} %collective-permute-done.7, ...), kind=kLoop, calls=%fused_computation.23 | loop fusion | flops 4423680 | bytes 6815744 | tf_op jit(solution)/shard_map/concatenate | solution.py:23
  178.8 7.4 %collective-permute-done.22 = f32[2,4,32,256]{3,2,1,0:T(8,128)S(1)} collective-permute-done((f32[2,4,32,256]{3,2,1,0:T(8,128)S(1)}, f32[2,4,32,256]{3,2,1,0:T(8,128)S(1)}, u32[]{:S(2)}, u32[]{:S(2)}) %collective-permute-start.22) | collective-permute-done | bytes 262176 | tf_op jit(solution)/shard_map/ppermute | solution.py:30
  186.4 7.3 %collective-permute-done.23 = f32[1,4,32,256]{3,2,1,0:T(8,128)S(1)} collective-permute-done((f32[1,4,32,256]{3,2,1,0:T(8,128)S(1)}, f32[1,4,32,256]{3,2,1,0:T(8,128)S(1)}, u32[]{:S(2)}, u32[]{:S(2)}) %collective-permute-start.23) | collective-permute-done | bytes 131104 | tf_op jit(solution)/shard_map/ppermute | solution.py:30
  (122 shorter events, 42.8 us)
Async XLA Ops:
  0.8 25.3 %collective-permute-start.1 = (f32[1,32,256]{2,1,0:T(8,128)S(1)}, f32[1,32,256]{2,1,0:T(8,128)S(1)}, u32[]{:S(2)}, u32[]{:S(2)}) collective-permute-start(f32[1,32,256]{2,1,0:T(8,128)S(1)} %get-tuple-element.64), channel_id=1, source_target_pairs={{0,64},{64,128},{128,192},{1,65},{65,129},{129,193},{2,66},{66,130... | collective-permute-start | bytes 98312 | tf_op jit(solution)/shard_map/ppermute | solution.py:19
  3.9 22.3 %collective-permute-start = (f32[1,32,256]{2,1,0:T(8,128)S(1)}, f32[1,32,256]{2,1,0:T(8,128)S(1)}, u32[]{:S(2)}, u32[]{:S(2)}) collective-permute-start(f32[1,32,256]{2,1,0:T(8,128)S(1)} %get-tuple-element.63), channel_id=1, source_target_pairs={{64,0},{128,64},{192,128},{65,1},{129,65},{193,129},{66,2},{130,66... | collective-permute-start | bytes 98312 | tf_op jit(solution)/shard_map/ppermute | solution.py:22
  26.2 8.6 %collective-permute-start.3 = (f32[6,1,256]{2,1,0:T(1,128)S(1)}, f32[6,1,256]{2,1,0:T(1,128)S(1)}, u32[]{:S(2)}, u32[]{:S(2)}) collective-permute-start(f32[6,1,256]{2,1,0:T(1,128)S(1)} %get-tuple-element.47), channel_id=1, source_target_pairs={{0,4},{4,8},{8,12},{12,16},{16,20},{20,24},{24,28},{28,32},{32,36}... | collective-permute-start | bytes 18440 | tf_op jit(solution)/shard_map/ppermute | solution.py:19
  28.1 6.6 %collective-permute-start.2 = (f32[6,1,256]{2,1,0:T(1,128)S(1)}, f32[6,1,256]{2,1,0:T(1,128)S(1)}, u32[]{:S(2)}, u32[]{:S(2)}) collective-permute-start(f32[6,1,256]{2,1,0:T(1,128)S(1)} %get-tuple-element.46), channel_id=1, source_target_pairs={{4,0},{8,4},{12,8},{16,12},{20,16},{24,20},{28,24},{32,28},{36,32}... | collective-permute-start | bytes 18440 | tf_op jit(solution)/shard_map/ppermute | solution.py:22
  34.9 11.2 %collective-permute-start.5 = (f32[6,34,1]{2,1,0:T(8,128)S(1)}, f32[6,34,1]{2,1,0:T(8,128)S(1)}, u32[]{:S(2)}, u32[]{:S(2)}) collective-permute-start(f32[6,34,1]{2,1,0:T(8,128)S(1)} %get-tuple-element.45), channel_id=1, source_target_pairs={{0,1},{1,2},{2,3},{4,5},{5,6},{6,7},{8,9},{9,10},{10,11},{12,13},{... | collective-permute-start | bytes 2456 | tf_op jit(solution)/shard_map/ppermute | solution.py:19
  36.4 9.8 %collective-permute-start.4 = (f32[6,34,1]{2,1,0:T(8,128)S(1)}, f32[6,34,1]{2,1,0:T(8,128)S(1)}, u32[]{:S(2)}, u32[]{:S(2)}) collective-permute-start(f32[6,34,1]{2,1,0:T(8,128)S(1)} %get-tuple-element.44), channel_id=1, source_target_pairs={{1,0},{2,1},{3,2},{5,4},{6,5},{7,6},{9,8},{10,9},{11,10},{13,12},{... | collective-permute-start | bytes 2456 | tf_op jit(solution)/shard_map/ppermute | solution.py:22
  48.3 16.5 %collective-permute-start.7 = (f32[4,4,16,256]{3,2,1,0:T(8,128)S(1)}, f32[4,4,16,256]{3,2,1,0:T(8,128)S(1)}, u32[]{:S(2)}, u32[]{:S(2)}) collective-permute-start(f32[4,4,16,256]{3,2,1,0:T(8,128)S(1)} %get-tuple-element.35), channel_id=1, source_target_pairs={{4,0},{8,4},{12,8},{16,12},{20,16},{24,20},{28,24},{32,28},{36,32}... | collective-permute-start | bytes 786440 | tf_op jit(solution)/shard_map/ppermute | solution.py:22
  50.2 19.4 %collective-permute-start.6 = (f32[4,4,16,256]{3,2,1,0:T(8,128)S(1)}, f32[4,4,16,256]{3,2,1,0:T(8,128)S(1)}, u32[]{:S(2)}, u32[]{:S(2)}) collective-permute-start(f32[4,4,16,256]{3,2,1,0:T(8,128)S(1)} %get-tuple-element.34), channel_id=1, source_target_pairs={{0,4},{4,8},{8,12},{12,16},{16,20},{20,24},{24,28},{28,32},{32,36}... | collective-permute-start | bytes 786440 | tf_op jit(solution)/shard_map/ppermute | solution.py:19
  54.3 17.3 %collective-permute-start.11 = (f32[4,4,16,256]{3,2,1,0:T(8,128)S(1)}, f32[4,4,16,256]{3,2,1,0:T(8,128)S(1)}, u32[]{:S(2)}, u32[]{:S(2)}) collective-permute-start(f32[4,4,16,256]{3,2,1,0:T(8,128)S(1)} %get-tuple-element.55), channel_id=1, source_target_pairs={{4,0},{8,4},{12,8},{16,12},{20,16},{24,20},{28,24},{32,28},{36,32}... | collective-permute-start | bytes 786440 | tf_op jit(solution)/shard_map/ppermute | solution.py:22
  58.0 60.0 %collective-permute-start.10 = (f32[4,4,16,256]{3,2,1,0:T(8,128)}, f32[4,4,16,256]{3,2,1,0:T(8,128)S(1)}, u32[]{:S(2)}, u32[]{:S(2)}) collective-permute-start(f32[4,4,16,256]{3,2,1,0:T(8,128)} %get-tuple-element.56), channel_id=1, source_target_pairs={{0,4},{4,8},{8,12},{12,16},{16,20},{20,24},{24,28},{28,32},{32,36}... | collective-permute-start | bytes 786440 | tf_op jit(solution)/shard_map/ppermute | solution.py:19
  62.8 55.2 %collective-permute-start.15 = (f32[4,4,16,256]{3,2,1,0:T(8,128)}, f32[4,4,16,256]{3,2,1,0:T(8,128)S(1)}, u32[]{:S(2)}, u32[]{:S(2)}) collective-permute-start(f32[4,4,16,256]{3,2,1,0:T(8,128)} %get-tuple-element.57), channel_id=1, source_target_pairs={{4,0},{8,4},{12,8},{16,12},{20,16},{24,20},{28,24},{32,28},{36,32}... | collective-permute-start | bytes 786440 | tf_op jit(solution)/shard_map/ppermute | solution.py:22
  64.8 53.2 %collective-permute-start.14 = (f32[4,4,16,256]{3,2,1,0:T(8,128)}, f32[4,4,16,256]{3,2,1,0:T(8,128)}, u32[]{:S(2)}, u32[]{:S(2)}) collective-permute-start(f32[4,4,16,256]{3,2,1,0:T(8,128)} %get-tuple-element.58), channel_id=1, source_target_pairs={{0,4},{4,8},{8,12},{12,16},{16,20},{20,24},{24,28},{28,32},{32,36}... | collective-permute-start | bytes 786440 | tf_op jit(solution)/shard_map/ppermute | solution.py:19
  69.6 48.4 %collective-permute-start.19 = (f32[4,4,16,256]{3,2,1,0:T(8,128)}, f32[4,4,16,256]{3,2,1,0:T(8,128)S(1)}, u32[]{:S(2)}, u32[]{:S(2)}) collective-permute-start(f32[4,4,16,256]{3,2,1,0:T(8,128)} %get-tuple-element.59), channel_id=1, source_target_pairs={{4,0},{8,4},{12,8},{16,12},{20,16},{24,20},{28,24},{32,28},{36,32}... | collective-permute-start | bytes 786440 | tf_op jit(solution)/shard_map/ppermute | solution.py:22
  71.6 46.4 %collective-permute-start.18 = (f32[4,4,16,256]{3,2,1,0:T(8,128)}, f32[4,4,16,256]{3,2,1,0:T(8,128)S(1)}, u32[]{:S(2)}, u32[]{:S(2)}) collective-permute-start(f32[4,4,16,256]{3,2,1,0:T(8,128)} %get-tuple-element.60), channel_id=1, source_target_pairs={{0,4},{4,8},{8,12},{12,16},{16,20},{20,24},{24,28},{28,32},{32,36}... | collective-permute-start | bytes 786440 | tf_op jit(solution)/shard_map/ppermute | solution.py:19
  119.6 15.1 %collective-permute-start.21 = (f32[4,4,64,16]{3,2,1,0:T(8,128)S(1)}, f32[4,4,64,16]{3,2,1,0:T(8,128)S(1)}, u32[]{:S(2)}, u32[]{:S(2)}) collective-permute-start(f32[4,4,64,16]{3,2,1,0:T(8,128)S(1)} %get-tuple-element.30), channel_id=1, source_target_pairs={{1,0},{2,1},{3,2},{5,4},{6,5},{7,6},{9,8},{10,9},{11,10},{13,12},{... | collective-permute-start | bytes 196616 | tf_op jit(solution)/shard_map/ppermute | solution.py:22
  122.3 14.9 %collective-permute-start.20 = (f32[4,4,64,16]{3,2,1,0:T(8,128)S(1)}, f32[4,4,64,16]{3,2,1,0:T(8,128)S(1)}, u32[]{:S(2)}, u32[]{:S(2)}) collective-permute-start(f32[4,4,64,16]{3,2,1,0:T(8,128)S(1)} %get-tuple-element.29), channel_id=1, source_target_pairs={{0,1},{1,2},{2,3},{4,5},{5,6},{6,7},{8,9},{9,10},{10,11},{12,13},{... | collective-permute-start | bytes 196616 | tf_op jit(solution)/shard_map/ppermute | solution.py:19
  123.8 19.9 %collective-permute-start.9 = (f32[4,4,64,16]{3,2,1,0:T(8,128)S(1)}, f32[4,4,64,16]{3,2,1,0:T(8,128)S(1)}, u32[]{:S(2)}, u32[]{:S(2)}) collective-permute-start(f32[4,4,64,16]{3,2,1,0:T(8,128)S(1)} %get-tuple-element.24), channel_id=1, source_target_pairs={{1,0},{2,1},{3,2},{5,4},{6,5},{7,6},{9,8},{10,9},{11,10},{13,12},{... | collective-permute-start | bytes 196616 | tf_op jit(solution)/shard_map/ppermute | solution.py:22
  128.4 20.1 %collective-permute-start.8 = (f32[4,4,64,16]{3,2,1,0:T(8,128)S(1)}, f32[4,4,64,16]{3,2,1,0:T(8,128)S(1)}, u32[]{:S(2)}, u32[]{:S(2)}) collective-permute-start(f32[4,4,64,16]{3,2,1,0:T(8,128)S(1)} %get-tuple-element.23), channel_id=1, source_target_pairs={{0,1},{1,2},{2,3},{4,5},{5,6},{6,7},{8,9},{9,10},{10,11},{12,13},{... | collective-permute-start | bytes 196616 | tf_op jit(solution)/shard_map/ppermute | solution.py:19
  129.9 25.1 %collective-permute-start.13 = (f32[4,4,64,16]{3,2,1,0:T(8,128)S(1)}, f32[4,4,64,16]{3,2,1,0:T(8,128)S(1)}, u32[]{:S(2)}, u32[]{:S(2)}) collective-permute-start(f32[4,4,64,16]{3,2,1,0:T(8,128)S(1)} %get-tuple-element.26), channel_id=1, source_target_pairs={{1,0},{2,1},{3,2},{5,4},{6,5},{7,6},{9,8},{10,9},{11,10},{13,12},{... | collective-permute-start | bytes 196616 | tf_op jit(solution)/shard_map/ppermute | solution.py:22
  134.7 25.0 %collective-permute-start.12 = (f32[4,4,64,16]{3,2,1,0:T(8,128)S(1)}, f32[4,4,64,16]{3,2,1,0:T(8,128)S(1)}, u32[]{:S(2)}, u32[]{:S(2)}) collective-permute-start(f32[4,4,64,16]{3,2,1,0:T(8,128)S(1)} %get-tuple-element.25), channel_id=1, source_target_pairs={{0,1},{1,2},{2,3},{4,5},{5,6},{6,7},{8,9},{9,10},{10,11},{12,13},{... | collective-permute-start | bytes 196616 | tf_op jit(solution)/shard_map/ppermute | solution.py:19
  137.3 29.0 %collective-permute-start.17 = (f32[4,4,64,16]{3,2,1,0:T(8,128)S(1)}, f32[4,4,64,16]{3,2,1,0:T(8,128)S(1)}, u32[]{:S(2)}, u32[]{:S(2)}) collective-permute-start(f32[4,4,64,16]{3,2,1,0:T(8,128)S(1)} %get-tuple-element.28), channel_id=1, source_target_pairs={{1,0},{2,1},{3,2},{5,4},{6,5},{7,6},{9,8},{10,9},{11,10},{13,12},{... | collective-permute-start | bytes 196616 | tf_op jit(solution)/shard_map/ppermute | solution.py:22
  143.8 27.2 %collective-permute-start.16 = (f32[4,4,64,16]{3,2,1,0:T(8,128)S(1)}, f32[4,4,64,16]{3,2,1,0:T(8,128)S(1)}, u32[]{:S(2)}, u32[]{:S(2)}) collective-permute-start(f32[4,4,64,16]{3,2,1,0:T(8,128)S(1)} %get-tuple-element.27), channel_id=1, source_target_pairs={{0,1},{1,2},{2,3},{4,5},{5,6},{6,7},{8,9},{9,10},{10,11},{12,13},{... | collective-permute-start | bytes 196616 | tf_op jit(solution)/shard_map/ppermute | solution.py:19
  177.5 8.7 %collective-permute-start.22 = (f32[2,4,32,256]{3,2,1,0:T(8,128)S(1)}, f32[2,4,32,256]{3,2,1,0:T(8,128)S(1)}, u32[]{:S(2)}, u32[]{:S(2)}) collective-permute-start(f32[2,4,32,256]{3,2,1,0:T(8,128)S(1)} %fusion.37), channel_id=1, source_target_pairs={{0,64},{64,0},{128,192},{192,128},{1,65},{65,1},{129,193},{193,129... | collective-permute-start | bytes 786440 | tf_op jit(solution)/shard_map/ppermute | solution.py:30
  186.3 7.4 %collective-permute-start.23 = (f32[1,4,32,256]{3,2,1,0:T(8,128)S(1)}, f32[1,4,32,256]{3,2,1,0:T(8,128)S(1)}, u32[]{:S(2)}, u32[]{:S(2)}) collective-permute-start(f32[1,4,32,256]{3,2,1,0:T(8,128)S(1)} %get-tuple-element.42), channel_id=1, source_target_pairs={{0,128},{64,192},{128,0},{192,64},{1,129},{65,193},{129,1},{193,65... | collective-permute-start | bytes 393224 | tf_op jit(solution)/shard_map/ppermute | solution.py:30
  (4 other events, 36.2 us)
where the time goes:
time: 196 us; the launch traced here: 194 us
  starting transfers between devices  65.4 us (33%)
  between operations  48.1 us (25%)
  waiting for transfers between devices  43.9 us (22%)
  local copies, waits for them, and re-layouts  14.7 us (8%)
  matrix products  11.4 us (6%)
  other arithmetic  10.8 us (6%)
    ppermute x11, starting transfers between devices, with_halo(): lax.ppermute(lax.slice_in_dim(block, 0, width, axis=dim), axis, backward)  33.8 us
    ppermute x11, starting transfers between devices, with_halo(): lax.ppermute(lax.slice_in_dim(block, block.shape[dim] - width, None, axis...  30.3 us
    ppermute x11, waiting for transfers between devices, with_halo(): lax.ppermute(lax.slice_in_dim(block, 0, width, axis=dim), axis, backward)  15.2 us
    ppermute x2, waiting for transfers between devices, swapped(): return lax.ppermute(value, axis, pairs)  14.6 us
    ppermute x11, waiting for transfers between devices, with_halo(): lax.ppermute(lax.slice_in_dim(block, block.shape[dim] - width, None, axis...  14 us
    dot_general x4, matrix products, table_lookup(): jnp.dot(tables, onehot, precision=lax.Precision.HIGHEST, preferred_elemen...  11.4 us
    slice x16, local copies, waits for them, and re-layouts, composite_view(): starts = (jnp.int32(0), MAXS - offset_pair[0], MAXS - offset_pair[1])  9.04 us
    concatenate x4, other arithmetic, with_halo(): block = jnp.concatenate([low, block, high], axis=dim)  5.78 us
  transfers between devices with their start and end apart: 24, of which 9 were waited for; matrix products, arithmetic and copies ran while one was open for 13% of the time, Pallas kernels for 0%

commit v1 on v0

v1 whole, which is shorter than its diff:
```python
import functools

import jax
import jax.numpy as jnp
from jax import lax
from jax.experimental import pallas as pl
from jax.experimental.pallas import tpu as pltpu
from jax.sharding import PartitionSpec as P

VIEWS = 4
MAXS = 16
SLICES = 4
ROWS = 32
COLS = 256
LANES = 128
EXT = ROWS + 2 * MAXS
FRAME = EXT + 16

ambient = 0.3
diffuse = 0.7

VMEM = pl.BlockSpec(memory_space=pltpu.VMEM)
SMEM = pl.BlockSpec(memory_space=pltpu.SMEM)
PARAMS = pltpu.CompilerParams(vmem_limit_bytes=32 * 1024 * 1024)


def f32(*shape):
    return jax.ShapeDtypeStruct(shape, jnp.float32)


def roll(value, shift):
    shift = shift % LANES
    return pltpu.roll(value, shift, 1) if shift else value


def lane_iota(rows):
    return lax.broadcasted_iota(jnp.int32, (rows, LANES), 1)


def pack_rows(density, index, last, first):
    for target, start, extra in ((last, ROWS - MAXS, ROWS - MAXS - 1), (first, 0, MAXS)):
        for s in range(SLICES):
            target[MAXS * s : MAXS * (s + 1)] = density[s, start : start + MAXS]
            target[EXT + MAXS * s : EXT + MAXS * (s + 1)] = index[s, start : start + MAXS].astype(
                jnp.float32
            )
        target[2 * EXT :] = jnp.zeros((8, COLS), jnp.float32)
        for s in range(SLICES):
            target[2 * EXT + s : 2 * EXT + s + 1] = density[s, extra : extra + 1]


def inside(axis):
    place = lax.axis_index(axis)
    return place > 0, place < lax.axis_size(axis) - 1


def tall(own, top, bottom, plane, keep, lanes):
    above = top[MAXS * plane : MAXS * (plane + 1), lanes]
    below = bottom[MAXS * plane : MAXS * (plane + 1), lanes]
    if keep is not None:
        above = jnp.where(keep[0], above, 0.0)
        below = jnp.where(keep[1], below, 0.0)
    return jnp.concatenate([above, own, below], axis=0)


def outer_rows(top, bottom, s, keep, lanes):
    above = jnp.where(keep[0], top[2 * EXT + s : 2 * EXT + s + 1, lanes], 0.0)
    below = jnp.where(keep[1], bottom[2 * EXT + s : 2 * EXT + s + 1, lanes], 0.0)
    sub = lax.broadcasted_iota(jnp.int32, (8, LANES), 0)
    return jnp.where(sub == 7, above, below)


def pack_cols(density, index, top, bottom, last, first):
    keep = inside("gx")
    lane = lane_iota(8)
    for target, lanes, turn, edge in (
        (last, slice(LANES, 2 * LANES), MAXS, LANES - MAXS - 1),
        (first, slice(0, LANES), 0, MAXS),
    ):
        main = [jnp.zeros((8, LANES), jnp.float32) for _ in range(9)]
        outer = [jnp.zeros((8, LANES), jnp.float32) for _ in range(2)]
        for plane in range(2 * SLICES):
            s = plane % SLICES
            if plane < SLICES:
                block = tall(density[s, :, lanes], top, bottom, plane, keep, lanes)
                block = jnp.concatenate([block, outer_rows(top, bottom, s, keep, lanes)], axis=0)
            else:
                block = tall(index[s, :, lanes].astype(jnp.float32), top, bottom, plane, None, lanes)
            mine = (lane >= MAXS * plane) & (lane < MAXS * (plane + 1))
            for t in range(block.shape[0] // 8):
                main[t] = jnp.where(mine, roll(block[8 * t : 8 * t + 8], MAXS * plane + turn), main[t])
            if plane < SLICES:
                for t in range(8):
                    shift = MAXS * plane + turn + t // 2
                    here = lane == (edge + shift) % LANES
                    outer[t % 2] = jnp.where(here, roll(block[8 * t : 8 * t + 8], shift), outer[t % 2])
        for t, value in enumerate(main + outer):
            target[8 * t : 8 * t + 8] = value


def assemble(density, index, top, bottom, left, right, frame, codes, first, last):
    keep = inside("gx")
    keep_left, keep_right = inside("gy")
    lane = lane_iota(8)
    from_left = lane >= LANES - MAXS - 1
    for s in range(SLICES):
        for k in range(2):
            lanes = slice(LANES * k, LANES * (k + 1))
            frame[s, k, 8 : 8 + EXT] = tall(density[s, :, lanes], top, bottom, s, keep, lanes)
            ends = outer_rows(top, bottom, s, keep, lanes)
            frame[s, k, 0:8] = ends
            frame[s, k, 8 + EXT :] = ends
            codes[s, k] = tall(
                index[s, :, lanes].astype(jnp.float32), top, bottom, SLICES + s, None, lanes
            ).astype(jnp.int32)
        for t in range(9):
            rows = slice(8 * t, 8 * t + 8)
            low = roll(left[rows], LANES - MAXS - MAXS * s)
            high = roll(right[rows], -MAXS * s)
            if t < 8:
                rest = slice(72 + 8 * (t % 2), 80 + 8 * (t % 2))
                outer = roll(left[rest], LANES - MAXS - MAXS * s - t // 2)
                low = jnp.where(lane == LANES - MAXS - 1, outer, low)
                outer = roll(right[rest], -MAXS * s - t // 2)
                high = jnp.where(lane == MAXS, outer, high)
            low = jnp.where(keep_left & from_left, low, 0.0)
            side = jnp.where(keep_right & (lane <= MAXS), high, low)
            if t < 8:
                frame[s, 2, 8 + 8 * t : 16 + 8 * t] = side
                low = roll(left[rows], LANES - MAXS - MAXS * (SLICES + s))
                high = roll(right[rows], -MAXS * (SLICES + s))
                value = jnp.where(lane < MAXS, high, jnp.where(from_left, low, 0.0))
                codes[s, 2, rows] = value.astype(jnp.int32)
            else:
                frame[s, 2, 0:8] = side
                frame[s, 2, 8 + EXT :] = side
    first[...] = frame[0, :, 8 : 8 + EXT]
    last[...] = frame[SLICES - 1, :, 8 : 8 + EXT]


def look_up(tables, code):
    low = code & (LANES - 1)
    under = code < LANES
    values = []
    for c in range(4):
        halves = [
            jnp.take_along_axis(
                jnp.broadcast_to(tables[c : c + 1, LANES * h : LANES * (h + 1)], code.shape),
                low,
                axis=1,
                mode="promise_in_bounds",
            )
            for h in range(2)
        ]
        values.append(jnp.where(under, *halves))
    return values


def shade(frame, codes, before, after, opacity, colors, light, shear, *refs):
    images, (scaled, alphas, bases) = refs[:VIEWS], refs[VIEWS:]
    depth_pos = lax.axis_index("depth")
    keep_before, keep_after = inside("depth")
    tables = jnp.concatenate([opacity[...], colors[...]], axis=0)
    lane = lane_iota(8)
    for s in range(SLICES):

        def row_tile(t, carry, s=s):
            at = pl.multiple_of(8 * t, 8)
            here = [frame[s, k, pl.ds(at + 8, 8)] for k in range(3)]
            to_right = [roll(value, 1) for value in here]
            to_left = [roll(value, -1) for value in here]
            for k in range(3):
                rows = (k, pl.ds(at, 8))
                if s == 0:
                    front = jnp.where(keep_before, before[rows], 0.0)
                else:
                    front = frame[s - 1, k, pl.ds(at + 8, 8)]
                if s == SLICES - 1:
                    back = jnp.where(keep_after, after[rows], 0.0)
                else:
                    back = frame[s + 1, k, pl.ds(at + 8, 8)]
                slope_depth = 0.5 * (back - front)
                slope_row = 0.5 * (
                    frame[s, k, pl.ds(at + 9, 8)] - frame[s, k, pl.ds(at + 7, 8)]
                )
                before_col = jnp.where(lane == 0, to_right[k - 1], to_right[k])
                after_col = jnp.where(lane == LANES - 1, to_left[(k + 1) % 3], to_left[k])
                slope_col = 0.5 * (after_col - before_col)
                scale = diffuse * lax.rsqrt(
                    slope_depth * slope_depth + slope_row * slope_row + slope_col * slope_col + 1.0
                )
                scaled[s, 0, *rows] = slope_depth * scale
                scaled[s, 1, *rows] = slope_row * scale
                scaled[s, 2, *rows] = slope_col * scale
                kappa, *color = look_up(tables, codes[s, *rows])
                alpha = 1.0 - jnp.exp(-kappa * here[k])
                alphas[s, *rows] = alpha
                for c in range(3):
                    bases[s, c, *rows] = alpha * color[c]
            return carry

        lax.fori_loop(0, EXT // 8, row_tile, 0)

    for k in range(VIEWS):
        view = depth_pos ^ k
        image = images[k]
        lights = [light[view, c] for c in range(3)]

        def row_tile(t, carry, view=view, image=image, lights=lights):
            accum = [[jnp.zeros((8, LANES), jnp.float32)] * 2 for _ in range(4)]
            for s in range(SLICES):
                shift_row = shear[view, depth_pos * SLICES + s, 0]
                shift_col = shear[view, depth_pos * SLICES + s, 1]
                turn = jnp.where(shift_col < 0, shift_col + LANES, shift_col)
                low = lane < shift_col
                high = lane > shift_col + (LANES - 1)
                start = 8 * t + MAXS - shift_row
                channels = [[], [], [], []]
                for j in range(3):
                    rows = (j, pl.ds(start, 8))
                    gain = ambient + jnp.abs(
                        lights[0] * scaled[s, 0, *rows]
                        + lights[1] * scaled[s, 1, *rows]
                        + lights[2] * scaled[s, 2, *rows]
                    )
                    channels[0].append(pltpu.roll(alphas[s, *rows], turn, 1))
                    for c in range(3):
                        channels[c + 1].append(pltpu.roll(bases[s, c, *rows] * gain, turn, 1))
                moved = [
                    (
                        jnp.where(low, r2, jnp.where(high, r1, r0)),
                        jnp.where(low, r0, jnp.where(high, r2, r1)),
                    )
                    for r0, r1, r2 in channels
                ]
                clear = [1.0 - accum[0][h] for h in range(2)]
                accum = [
                    [accum[c][h] + clear[h] * moved[c][h] for h in range(2)] for c in range(4)
                ]
            rows = pl.ds(pl.multiple_of(8 * t, 8), 8)
            for c in range(4):
                for h in range(2):
                    image[c, rows, LANES * h : LANES * (h + 1)] = accum[c][h]
            return carry

        lax.fori_loop(0, ROWS // 8, row_tile, 0)


def merge(own, one, two, three, out):
    depth_pos = lax.axis_index("depth")
    odd = depth_pos % 2 == 1
    high = depth_pos >= 2

    def row_tile(t, carry):
        rows = pl.ds(pl.multiple_of(8 * t, 8), 8)

        def over(flip, near, far):
            front = [jnp.where(flip, b, a) for a, b in zip(near, far)]
            back = [jnp.where(flip, a, b) for a, b in zip(near, far)]
            clear = 1.0 - front[0]
            return [a + clear * b for a, b in zip(front, back)]

        for h in range(2):
            lanes = slice(LANES * h, LANES * (h + 1))
            parts = [[ref[c, rows, lanes] for c in range(4)] for ref in (own, one, two, three)]
            total = over(high, over(odd, parts[0], parts[1]), over(odd, parts[2], parts[3]))
            for c in range(4):
                out[0, c, rows, lanes] = total[c]
        return carry

    lax.fori_loop(0, ROWS // 8, row_tile, 0)


def call(kernel, ins, outs, scratch=(), cost=1000000):
    return pl.pallas_call(
        kernel,
        out_shape=outs,
        in_specs=ins,
        out_specs=[VMEM] * len(outs),
        scratch_shapes=scratch,
        compiler_params=PARAMS,
        cost_estimate=pl.CostEstimate(flops=cost, bytes_accessed=cost, transcendentals=0),
    )


def neighbours(to_next, to_previous, axis):
    count = lax.axis_size(axis)
    ahead = [(i, (i + 1) % count) for i in range(count)]
    return (
        lax.ppermute(to_next, axis, ahead),
        lax.ppermute(to_previous, axis, [(target, source) for source, target in ahead]),
    )


def local(density, table_index, opacity_table, color_table, light_direction, shear_offsets):
    strip = f32(2 * EXT + 8, COLS)
    last, first = call(pack_rows, [VMEM] * 2, [strip, strip])(density, table_index)
    top, bottom = neighbours(last, first, "gx")
    strip = f32(88, LANES)
    last, first = call(pack_cols, [VMEM] * 4, [strip, strip])(density, table_index, top, bottom)
    left, right = neighbours(last, first, "gy")
    frame, codes, first, last = call(
        assemble,
        [VMEM] * 6,
        [
            f32(SLICES, 3, FRAME, LANES),
            jax.ShapeDtypeStruct((SLICES, 3, EXT, LANES), jnp.int32),
            f32(3, EXT, LANES),
            f32(3, EXT, LANES),
        ],
    )(density, table_index, top, bottom, left, right)
    before, after = neighbours(last, first, "depth")
    images = call(
        shade,
        [VMEM] * 6 + [SMEM] * 2,
        [f32(4, ROWS, COLS)] * VIEWS,
        [
            pltpu.VMEM((SLICES, 3, 3, EXT, LANES), jnp.float32),
            pltpu.VMEM((SLICES, 3, EXT, LANES), jnp.float32),
            pltpu.VMEM((SLICES, 3, 3, EXT, LANES), jnp.float32),
        ],
    )(
        frame,
        codes,
        before,
        after,
        opacity_table[None],
        color_table,
        light_direction,
        shear_offsets,
    )
    received = [images[0]]
    for k in (1, 2, 3):
        received.append(lax.ppermute(images[k], "depth", [(i, i ^ k) for i in range(4)]))
    return call(merge, [VMEM] * 4, [f32(1, 4, ROWS, COLS)])(*received)[0]


def solution(mesh):
    return jax.shard_map(
        local,
        mesh=mesh,
        in_specs=(P("depth", "gx", "gy"), P("depth", "gx", "gy"), P(), P(), P(), P()),
        out_specs=P("depth", None, "gx", "gy"),
        check_vma=False,
    )
```

time: 196 us -> 42 us (0.21)
  the two profiles are of different devices: /device:TPU:124 before, /device:TPU:97 now
where the time goes in v1:
time: 42 us; the launch traced here: 41.8 us
  waiting for transfers between devices  17.9 us (43%)
  starting transfers between devices  13 us (31%)
  Pallas kernels  8.3 us (20%)
  local copies, waits for them, and re-layouts  2.58 us (6%)
    ppermute x3, waiting for transfers between devices, local(): lax.ppermute(images[k], 'depth', [(i, i ^ k) for i in range(4)])  8.94 us
    pallas_call x1, Pallas kernels, local(): call(shade, [VMEM] * 6 + [SMEM] * 2, [f32(4, ROWS, COLS)] * VIEWS, [pltpu...  7.03 us
    ppermute x3, starting transfers between devices, neighbours(): lax.ppermute(to_next, axis, ahead)  6.08 us
    ppermute x3, waiting for transfers between devices, neighbours(): lax.ppermute(to_next, axis, ahead)  5.26 us
    ppermute x3, starting transfers between devices, local(): lax.ppermute(images[k], 'depth', [(i, i ^ k) for i in range(4)])  3.94 us
    ppermute x3, waiting for transfers between devices, neighbours(): lax.ppermute(to_previous, axis, [(target, source) for source, target in a...  3.69 us
    ppermute x3, starting transfers between devices, neighbours(): lax.ppermute(to_previous, axis, [(target, source) for source, target in a...  2.99 us
    unnamed x13, local copies, waits for them, and re-layouts  2.58 us
  transfers between devices with their start and end apart: 9, of which 7 were waited for; matrix products, arithmetic and copies ran while one was open for 0% of the time, Pallas kernels for 0%

profile of v1, /device:TPU:97, one launch (start us, length us, event | category | flops | bytes accessed | tf_op | source)
XLA Modules:
  0.0 41.8 jit_solution(12034105052362786961)
XLA Ops:
  0.0 0.9 %copy-done = f32[4,32,256]{2,1,0:T(8,128)S(1)} copy-done((f32[4,32,256]{2,1,0:T(8,128)S(1)}, f32[4,32,256]{2,1,0:T(8,128)}, u32[]{:S(2)}) %copy-start) | copy-done | bytes 131096
  0.9 0.9 %copy-done.1 = s32[4,32,256]{2,1,0:T(8,128)S(1)} copy-done((s32[4,32,256]{2,1,0:T(8,128)S(1)}, s32[4,32,256]{2,1,0:T(8,128)}, u32[]{:S(2)}) %copy-start.1) | copy-done | bytes 131096
  1.8 3.4 %collective-permute-start = (f32[136,256]{1,0:T(8,128)S(1)}, f32[136,256]{1,0:T(8,128)S(1)}, u32[]{:S(2)}, u32[]{:S(2)}) collective-permute-start(f32[136,256]{1,0:T(8,128)S(1)} %get-tuple-element.17), channel_id=1, source_target_pairs={{0,4},{4,8},{8,12},{12,16},{16,20},{20,24},{24,28},{28,32},{32,36}... | collective-permute-start | bytes 417800 | tf_op jit(solution)/shard_map/ppermute | solution.py:290
  5.3 2.0 %collective-permute-done.top = f32[136,256]{1,0:T(8,128)S(1)} collective-permute-done((f32[136,256]{1,0:T(8,128)S(1)}, f32[136,256]{1,0:T(8,128)S(1)}, u32[]{:S(2)}, u32[]{:S(2)}) %collective-permute-start) | collective-permute-done | bytes 139296 | tf_op jit(solution)/shard_map/ppermute | solution.py:290
  7.3 3.7 %collective-permute-done.1.bottom = f32[136,256]{1,0:T(8,128)S(1)} collective-permute-done((f32[136,256]{1,0:T(8,128)S(1)}, f32[136,256]{1,0:T(8,128)S(1)}, u32[]{:S(2)}, u32[]{:S(2)}) %collective-permute-start.1) | collective-permute-done | bytes 139296 | tf_op jit(solution)/shard_map/ppermute | solution.py:291
  10.9 0.2 shard_map.65
  11.2 1.4 %collective-permute-start.2 = (f32[88,128]{1,0:T(8,128)S(1)}, f32[88,128]{1,0:T(8,128)S(1)}, u32[]{:S(2)}, u32[]{:S(2)}) collective-permute-start(f32[88,128]{1,0:T(8,128)S(1)} %get-tuple-element.19), channel_id=1, source_target_pairs={{0,1},{1,2},{2,3},{3,0},{4,5},{5,6},{6,7},{7,4},{8,9},{9,10},{10,1... | collective-permute-start | bytes 135176 | tf_op jit(solution)/shard_map/ppermute | solution.py:290
  12.6 1.5 %collective-permute-start.3 = (f32[88,128]{1,0:T(8,128)S(1)}, f32[88,128]{1,0:T(8,128)S(1)}, u32[]{:S(2)}, u32[]{:S(2)}) collective-permute-start(f32[88,128]{1,0:T(8,128)S(1)} %get-tuple-element.20), channel_id=1, source_target_pairs={{1,0},{2,1},{3,2},{0,3},{5,4},{6,5},{7,6},{4,7},{9,8},{10,9},{11,1... | collective-permute-start | bytes 135176 | tf_op jit(solution)/shard_map/ppermute | solution.py:291
  14.1 1.3 %collective-permute-done.2.left = f32[88,128]{1,0:T(8,128)S(1)} collective-permute-done((f32[88,128]{1,0:T(8,128)S(1)}, f32[88,128]{1,0:T(8,128)S(1)}, u32[]{:S(2)}, u32[]{:S(2)}) %collective-permute-start.2) | collective-permute-done | bytes 45088 | tf_op jit(solution)/shard_map/ppermute | solution.py:290
  15.5 0.0 collective-permute-done.3.right
  15.5 0.3 shard_map.66
  15.7 1.3 %collective-permute-start.4 = (f32[3,64,128]{2,1,0:T(8,128)S(1)}, f32[3,64,128]{2,1,0:T(8,128)S(1)}, u32[]{:S(2)}, u32[]{:S(2)}) collective-permute-start(f32[3,64,128]{2,1,0:T(8,128)S(1)} %get-tuple-element.23), channel_id=1, source_target_pairs={{0,64},{64,128},{128,192},{192,0},{1,65},{65,129},{129,193},{193,1... | collective-permute-start | bytes 294920 | tf_op jit(solution)/shard_map/ppermute | solution.py:290
  17.0 1.5 %collective-permute-start.5 = (f32[3,64,128]{2,1,0:T(8,128)S(1)}, f32[3,64,128]{2,1,0:T(8,128)S(1)}, u32[]{:S(2)}, u32[]{:S(2)}) collective-permute-start(f32[3,64,128]{2,1,0:T(8,128)S(1)} %get-tuple-element.24), channel_id=1, source_target_pairs={{64,0},{128,64},{192,128},{0,192},{65,1},{129,65},{193,129},{1,193... | collective-permute-start | bytes 294920 | tf_op jit(solution)/shard_map/ppermute | solution.py:291
  18.5 0.1 copy.7.shear
  18.6 1.9 %collective-permute-done.4.before = f32[3,64,128]{2,1,0:T(8,128)S(1)} collective-permute-done((f32[3,64,128]{2,1,0:T(8,128)S(1)}, f32[3,64,128]{2,1,0:T(8,128)S(1)}, u32[]{:S(2)}, u32[]{:S(2)}) %collective-permute-start.4) | collective-permute-done | bytes 98336 | tf_op jit(solution)/shard_map/ppermute | solution.py:290
  20.5 0.7 %copy-done.4 = f32[256]{0:T(256)S(1)} copy-done((f32[256]{0:T(256)S(1)}, f32[256]{0:T(256)}, u32[]{:S(2)}) %copy-start.4) | copy-done | bytes 1048
  21.2 7.0 %shard_map.67 = (f32[4,32,256]{2,1,0:T(8,128)S(1)}, f32[4,32,256]{2,1,0:T(8,128)S(1)}, f32[4,32,256]{2,1,0:T(8,128)S(1)}, f32[4,32,256]{2,1,0:T(8,128)S(1)}) custom-call(f32[4,3,80,128]{3,2,1,0:T(8,128)S(1)} %get-tuple-element.21.frame, s32[4,3,64,128]{3,2,1,0:T(8,128)S(1)} %get-tuple-element.22.codes, f32[3,64,128]{2,1,0:T(8,128)S(1)} %collective-permute-done.4.before, ...), custom_call_target="tpu_custom_call" | custom-call | flops 1000000 | bytes 1000000 | tf_op jit(solution)/shard_map/pallas_call | solution.py:313
  28.2 1.3 %collective-permute-start.6 = (f32[4,32,256]{2,1,0:T(8,128)S(1)}, f32[4,32,256]{2,1,0:T(8,128)S(1)}, u32[]{:S(2)}, u32[]{:S(2)}) collective-permute-start(f32[4,32,256]{2,1,0:T(8,128)S(1)} %get-tuple-element.26), channel_id=1, source_target_pairs={{0,64},{64,0},{128,192},{192,128},{1,65},{65,1},{129,193},{193,129... | collective-permute-start | bytes 393224 | tf_op jit(solution)/shard_map/ppermute | solution.py:334
  29.5 2.6 %collective-permute-start.7 = (f32[4,32,256]{2,1,0:T(8,128)S(1)}, f32[4,32,256]{2,1,0:T(8,128)S(1)}, u32[]{:S(2)}, u32[]{:S(2)}) collective-permute-start(f32[4,32,256]{2,1,0:T(8,128)S(1)} %get-tuple-element.27), channel_id=1, source_target_pairs={{0,128},{64,192},{128,0},{192,64},{1,129},{65,193},{129,1},{193,65... | collective-permute-start | bytes 393224 | tf_op jit(solution)/shard_map/ppermute | solution.py:334
  32.2 0.0 collective-permute-start.8
  32.2 1.3 %collective-permute-done.6.one = f32[4,32,256]{2,1,0:T(8,128)S(1)} collective-permute-done((f32[4,32,256]{2,1,0:T(8,128)S(1)}, f32[4,32,256]{2,1,0:T(8,128)S(1)}, u32[]{:S(2)}, u32[]{:S(2)}) %collective-permute-start.6) | collective-permute-done | bytes 131104 | tf_op jit(solution)/shard_map/ppermute | solution.py:334
  33.5 4.7 %collective-permute-done.7.two = f32[4,32,256]{2,1,0:T(8,128)S(1)} collective-permute-done((f32[4,32,256]{2,1,0:T(8,128)S(1)}, f32[4,32,256]{2,1,0:T(8,128)S(1)}, u32[]{:S(2)}, u32[]{:S(2)}) %collective-permute-start.7) | collective-permute-done | bytes 131104 | tf_op jit(solution)/shard_map/ppermute | solution.py:334
  38.2 2.9 %collective-permute-done.8.three = f32[4,32,256]{2,1,0:T(8,128)S(1)} collective-permute-done((f32[4,32,256]{2,1,0:T(8,128)S(1)}, f32[4,32,256]{2,1,0:T(8,128)S(1)}, u32[]{:S(2)}, u32[]{:S(2)}) %collective-permute-start.8) | collective-permute-done | bytes 131104 | tf_op jit(solution)/shard_map/ppermute | solution.py:334
  41.1 0.7 %shard_map.68 = f32[1,4,32,256]{3,2,1,0:T(8,128)} custom-call(f32[4,32,256]{2,1,0:T(8,128)S(1)} %get-tuple-element.25.own, f32[4,32,256]{2,1,0:T(8,128)S(1)} %collective-permute-done.6.one, f32[4,32,256]{2,1,0:T(8,128)S(1)} %collective-permute-done.7.two, f32[4,32,256]{2,1,0:T(8,128)S(1)} %collective-permute-done.8.three), custom_call_target="tpu_custom_call" | custom-call | flops 1000000 | bytes 1000000 | tf_op jit(solution)/shard_map/pallas_call | solution.py:335
  (12 shorter events, 0.0 us)
Async XLA Ops:
  0.0 0.9 %copy-start = (f32[4,32,256]{2,1,0:T(8,128)S(1)}, f32[4,32,256]{2,1,0:T(8,128)}, u32[]{:S(2)}) copy-start(f32[4,32,256]{2,1,0:T(8,128)} %density.5) | copy-start | bytes 393220
  0.9 0.9 %copy-start.1 = (s32[4,32,256]{2,1,0:T(8,128)S(1)}, s32[4,32,256]{2,1,0:T(8,128)}, u32[]{:S(2)}) copy-start(s32[4,32,256]{2,1,0:T(8,128)} %index.5) | copy-start | bytes 393220
  1.8 5.4 %collective-permute-start = (f32[136,256]{1,0:T(8,128)S(1)}, f32[136,256]{1,0:T(8,128)S(1)}, u32[]{:S(2)}, u32[]{:S(2)}) collective-permute-start(f32[136,256]{1,0:T(8,128)S(1)} %get-tuple-element.17), channel_id=1, source_target_pairs={{0,4},{4,8},{8,12},{12,16},{16,20},{20,24},{24,28},{28,32},{32,36}... | collective-permute-start | bytes 417800 | tf_op jit(solution)/shard_map/ppermute | solution.py:290
  5.3 5.7 %collective-permute-start.1 = (f32[136,256]{1,0:T(8,128)S(1)}, f32[136,256]{1,0:T(8,128)S(1)}, u32[]{:S(2)}, u32[]{:S(2)}) collective-permute-start(f32[136,256]{1,0:T(8,128)S(1)} %get-tuple-element.18), channel_id=1, source_target_pairs={{4,0},{8,4},{12,8},{16,12},{20,16},{24,20},{28,24},{32,28},{36,32}... | collective-permute-start | bytes 417800 | tf_op jit(solution)/shard_map/ppermute | solution.py:291
  11.2 4.2 %collective-permute-start.2 = (f32[88,128]{1,0:T(8,128)S(1)}, f32[88,128]{1,0:T(8,128)S(1)}, u32[]{:S(2)}, u32[]{:S(2)}) collective-permute-start(f32[88,128]{1,0:T(8,128)S(1)} %get-tuple-element.19), channel_id=1, source_target_pairs={{0,1},{1,2},{2,3},{3,0},{4,5},{5,6},{6,7},{7,4},{8,9},{9,10},{10,1... | collective-permute-start | bytes 135176 | tf_op jit(solution)/shard_map/ppermute | solution.py:290
  12.6 2.9 %collective-permute-start.3 = (f32[88,128]{1,0:T(8,128)S(1)}, f32[88,128]{1,0:T(8,128)S(1)}, u32[]{:S(2)}, u32[]{:S(2)}) collective-permute-start(f32[88,128]{1,0:T(8,128)S(1)} %get-tuple-element.20), channel_id=1, source_target_pairs={{1,0},{2,1},{3,2},{0,3},{5,4},{6,5},{7,6},{4,7},{9,8},{10,9},{11,1... | collective-permute-start | bytes 135176 | tf_op jit(solution)/shard_map/ppermute | solution.py:291
  15.5 3.0 %copy-start.5 = (s32[4,16,2]{1,2,0:T(2,128)S(1)}, s32[4,16,2]{1,2,0:T(2,128)}, u32[]{:S(2)}) copy-start(s32[4,16,2]{1,2,0:T(2,128)} %param.11) | copy-start | bytes 1540
  15.7 4.8 %collective-permute-start.4 = (f32[3,64,128]{2,1,0:T(8,128)S(1)}, f32[3,64,128]{2,1,0:T(8,128)S(1)}, u32[]{:S(2)}, u32[]{:S(2)}) collective-permute-start(f32[3,64,128]{2,1,0:T(8,128)S(1)} %get-tuple-element.23), channel_id=1, source_target_pairs={{0,64},{64,128},{128,192},{192,0},{1,65},{65,129},{129,193},{193,1... | collective-permute-start | bytes 294920 | tf_op jit(solution)/shard_map/ppermute | solution.py:290
  17.0 3.5 %collective-permute-start.5 = (f32[3,64,128]{2,1,0:T(8,128)S(1)}, f32[3,64,128]{2,1,0:T(8,128)S(1)}, u32[]{:S(2)}, u32[]{:S(2)}) collective-permute-start(f32[3,64,128]{2,1,0:T(8,128)S(1)} %get-tuple-element.24), channel_id=1, source_target_pairs={{64,0},{128,64},{192,128},{0,192},{65,1},{129,65},{193,129},{1,193... | collective-permute-start | bytes 294920 | tf_op jit(solution)/shard_map/ppermute | solution.py:291
  18.5 2.0 %copy-start.3 = (f32[4,3]{1,0:T(4,128)S(1)}, f32[4,3]{1,0:T(4,128)}, u32[]{:S(2)}) copy-start(f32[4,3]{1,0:T(4,128)} %light.1) | copy-start | bytes 148
  18.6 1.9 %copy-start.2 = (f32[3,256]{1,0:T(4,128)S(1)}, f32[3,256]{1,0:T(4,128)}, u32[]{:S(2)}) copy-start(f32[3,256]{1,0:T(4,128)} %colors.1) | copy-start | bytes 9220
  20.5 0.7 %copy-start.4 = (f32[256]{0:T(256)S(1)}, f32[256]{0:T(256)}, u32[]{:S(2)}) copy-start(f32[256]{0:T(256)} %param.8) | copy-start | bytes 3076
  28.2 5.2 %collective-permute-start.6 = (f32[4,32,256]{2,1,0:T(8,128)S(1)}, f32[4,32,256]{2,1,0:T(8,128)S(1)}, u32[]{:S(2)}, u32[]{:S(2)}) collective-permute-start(f32[4,32,256]{2,1,0:T(8,128)S(1)} %get-tuple-element.26), channel_id=1, source_target_pairs={{0,64},{64,0},{128,192},{192,128},{1,65},{65,1},{129,193},{193,129... | collective-permute-start | bytes 393224 | tf_op jit(solution)/shard_map/ppermute | solution.py:334
  29.5 8.7 %collective-permute-start.7 = (f32[4,32,256]{2,1,0:T(8,128)S(1)}, f32[4,32,256]{2,1,0:T(8,128)S(1)}, u32[]{:S(2)}, u32[]{:S(2)}) collective-permute-start(f32[4,32,256]{2,1,0:T(8,128)S(1)} %get-tuple-element.27), channel_id=1, source_target_pairs={{0,128},{64,192},{128,0},{192,64},{1,129},{65,193},{129,1},{193,65... | collective-permute-start | bytes 393224 | tf_op jit(solution)/shard_map/ppermute | solution.py:334
  32.2 8.9 %collective-permute-start.8 = (f32[4,32,256]{2,1,0:T(8,128)S(1)}, f32[4,32,256]{2,1,0:T(8,128)S(1)}, u32[]{:S(2)}, u32[]{:S(2)}) collective-permute-start(f32[4,32,256]{2,1,0:T(8,128)S(1)} %get-tuple-element.28), channel_id=1, source_target_pairs={{0,192},{64,128},{128,64},{192,0},{1,193},{65,129},{129,65},{193,1... | collective-permute-start | bytes 393224 | tf_op jit(solution)/shard_map/ppermute | solution.py:334
